TPU v7x, 32 devices: a whole 2x2x4 slice. The times are simulated.
32 devices in a mesh: groups: 1, res: 16 (over z, y, core), sub: 2 (over x).
Axes of the slice: x: 2, y: 2, z: 4, core: 2. Of those that a mesh axis runs over, the one named last changes fastest.
Arguments:
- sequence_embedding: bfloat16 [16, 256, 64], P('sub', ('groups', 'res')), may hold values from -6 to 6
- sequence_present_flags: int32 [16, 256], P('sub', ('groups', 'res')), may hold values 0 or 1
- position_couple_flags: int32 [256, 256], P(('groups', 'res'), 'sub'), may hold values 0 or 1
- first_factor_matrix: bfloat16 [64, 32], replicated, may hold values from -0.75 to 0.75
- second_factor_matrix: bfloat16 [64, 32], replicated, may hold values from -0.75 to 0.75
- final_linear_matrix: bfloat16 [1024, 128], replicated, may hold values from -0.1875 to 0.1875
- final_offset_vector: float32 [128], replicated, may hold values from -3 to 3
- couple_change_cotangent: float32 [256, 256, 128], P(('groups', 'res'), 'sub'), may hold values from -6 to 6
Outputs:
- pair_delta_output: bfloat16 [256, 256, 128], P(('groups', 'res'), 'sub')
- alignment_gradient: float32 [16, 256, 64], P('sub', ('groups', 'res'))
- left_weight_gradient: float32 [64, 32], P('groups')
- right_weight_gradient: float32 [64, 32], P('groups')
- output_weight_gradient: float32 [1024, 128], P('groups')
- output_bias_gradient: float32 [128], P('groups')
All inputs are finite; a program needn't handle non-finite values. No bound on the sum of `sequence_present_flags` or of `position_couple_flags` on one device may be relied on, other than what follows from the above.
Results may differ from a plain program's by a relative error of at most 0.0074.
Values may be sent and summed in bfloat16 or wider, within the bound.
A program may use at most 64 MiB of HBM per device.

v0:
```python
import jax
import jax.numpy as jnp
from jax import lax
from jax.sharding import PartitionSpec as P


def body(
    sequence_embedding,
    sequence_present_flags,
    position_couple_flags,
    first_factor_matrix,
    second_factor_matrix,
    final_linear_matrix,
    final_offset_vector,
    couple_change_cotangent,
):
    highest = lax.Precision.HIGHEST
    precise_scalar = jnp.float32
    hidden = first_factor_matrix.shape[1]
    pair_width = final_linear_matrix.shape[1]
    position_span = sequence_embedding.shape[1]
    col_width = couple_change_cotangent.shape[1]
    col_start = lax.axis_index("sub") * col_width
    present_count_items = sequence_embedding.astype(precise_scalar)
    centred = present_count_items - jnp.mean(present_count_items, axis=-1, keepdims=True)
    variance = jnp.mean(centred * centred, axis=-1, keepdims=True)
    reciprocal_deviation = lax.rsqrt(variance + 1e-05)
    normalized_input = centred * reciprocal_deviation
    layer_scaled_half = normalized_input.astype(jnp.bfloat16)
    row_presence_mask = sequence_present_flags.astype(precise_scalar)[:, None, :]
    first_factor_features = jnp.einsum(
        "sim,mc->sci", layer_scaled_half, first_factor_matrix, preferred_element_type=precise_scalar
    )
    second_factor_features = jnp.einsum(
        "sim,mc->sci",
        layer_scaled_half,
        second_factor_matrix,
        preferred_element_type=precise_scalar,
    )
    feat_a = (first_factor_features * row_presence_mask).astype(jnp.bfloat16)
    feat_b = (second_factor_features * row_presence_mask).astype(jnp.bfloat16)
    mask16 = row_presence_mask.astype(jnp.bfloat16)
    all_a, all_b, all_mask = (
        lax.all_gather(feat_a, "sub", axis=0, tiled=True),
        lax.all_gather(feat_b, "sub", axis=0, tiled=True),
        lax.all_gather(mask16, "sub", axis=0, tiled=True),
    )
    wide_b, wide_mask = (
        lax.all_gather(all_b, "res", axis=2, tiled=True),
        lax.all_gather(all_mask, "res", axis=2, tiled=True),
    )
    col_b = lax.dynamic_slice_in_dim(wide_b, col_start, col_width, 2)
    col_mask = lax.dynamic_slice_in_dim(wide_mask, col_start, col_width, 2)
    pair_count = jnp.einsum(
        "sxi,sxj->ij", all_mask, col_mask, preferred_element_type=precise_scalar
    )
    divisor = jnp.maximum(pair_count, 1.0)[:, :, None]
    out_cube = final_linear_matrix.reshape(hidden, hidden, pair_width)
    tmix = jnp.einsum(
        "sci,cde->side", all_a, out_cube, preferred_element_type=precise_scalar
    ).astype(jnp.bfloat16)
    zsum = jnp.einsum("side,sdj->ije", tmix, col_b, preferred_element_type=precise_scalar)
    pmask = position_couple_flags.astype(precise_scalar)[:, :, None]
    pair_delta_output = (pmask * (zsum + final_offset_vector) / divisor).astype(jnp.bfloat16)
    gscaled32 = couple_change_cotangent * pmask / divisor
    bias_part = jnp.sum(gscaled32, axis=(0, 1))
    gscaled = gscaled32.astype(jnp.bfloat16)
    dtmix = jnp.einsum("ije,sdj->side", gscaled, col_b, preferred_element_type=precise_scalar)
    db_part = jnp.einsum("ije,side->sdj", gscaled, tmix, preferred_element_type=precise_scalar)
    cube_f32 = out_cube.astype(precise_scalar)
    da_part = jnp.einsum("side,cde->sci", dtmix, cube_f32, precision=highest)
    out_part = jnp.einsum("sci,side->cde", all_a.astype(precise_scalar), dtmix, precision=highest)
    placed = jnp.zeros((db_part.shape[0], hidden, wide_b.shape[2]), precise_scalar)
    placed = lax.dynamic_update_slice_in_dim(placed, db_part, col_start, 2)
    res_totals = lax.psum_scatter(placed, "res", scatter_dimension=2, tiled=True)
    da_rows, db_rows = (
        lax.psum_scatter(da_part, "sub", scatter_dimension=0, tiled=True),
        lax.psum_scatter(res_totals, "sub", scatter_dimension=0, tiled=True),
    )
    dfeat_a = da_rows * row_presence_mask
    dfeat_b = db_rows * row_presence_mask
    normed_f = layer_scaled_half.astype(precise_scalar)
    wa_part = jnp.einsum("sim,sci->mc", normed_f, dfeat_a, precision=highest)
    wb_part = jnp.einsum("sim,sci->mc", normed_f, dfeat_b, precision=highest)
    totals = lax.psum((out_part, bias_part, wa_part, wb_part), ("res", "sub"))
    inv_res = 1.0 / (position_span * lax.axis_size("res"))
    output_weight_gradient = totals[0].reshape(hidden * hidden, pair_width) * inv_res
    output_bias_gradient = totals[1] * inv_res
    left_weight_gradient = totals[2] * inv_res
    right_weight_gradient = totals[3] * inv_res
    normalized_gradient = jnp.einsum(
        "sci,mc->sim", dfeat_a, first_factor_matrix.astype(precise_scalar), precision=highest
    )
    normalized_gradient = normalized_gradient + jnp.einsum(
        "sci,mc->sim", dfeat_b, second_factor_matrix.astype(precise_scalar), precision=highest
    )
    alignment_gradient = reciprocal_deviation * (
        normalized_gradient
        - jnp.mean(normalized_gradient, axis=-1, keepdims=True)
        - normalized_input
        * jnp.mean(normalized_gradient * normalized_input, axis=-1, keepdims=True)
    )
    return (
        pair_delta_output,
        alignment_gradient,
        left_weight_gradient,
        right_weight_gradient,
        output_weight_gradient,
        output_bias_gradient,
    )


def solution(mesh):
    in_specs = (
        P("sub", ("groups", "res"), None),
        P("sub", ("groups", "res")),
        P(("groups", "res"), "sub"),
        P(),
        P(),
        P(),
        P(),
        P(("groups", "res"), "sub", None),
    )
    out_specs = (
        P(("groups", "res"), "sub", None),
        P("sub", ("groups", "res"), None),
        P("groups", None),
        P("groups", None),
        P("groups", None),
        P("groups"),
    )
    return jax.shard_map(body, mesh=mesh, in_specs=in_specs, out_specs=out_specs, check_vma=False)
```

profile of v0, /device:TPU:0, one launch (start us, length us, event | category | flops | bytes accessed | tf_op | source)
XLA Modules:
  0.0 273.6 jit_solution(4974861331396434097)
XLA Ops:
  8.0 0.0 copy-start
  8.0 0.0 reduce-scatter.4.cloned.1.call-start
  8.1 0.9 convert_reduce_fusion
  9.0 0.9 fusion.61
  10.0 0.7 convert_convert_fusion
  10.7 5.2 %all-gather = bf16[16,16]{1,0:T(8,128)(2,1)S(1)} all-gather(bf16[8,16]{1,0:T(8,128)(2,1)S(1)} %get-tuple-element.11), channel_id=2, replica_groups=mesh['groups'=1,'res'=16,'sub'=2] {'sub'}, dimensions={0}, use_global_device_ids=true | all-gather | bytes 768 | tf_op jit(solution)/shard_map/all_gather | solution.py:46
  15.9 0.1 copy.51
  16.0 0.7 convert_element_type.44
  16.7 1.0 fusion.41
  17.6 4.6 %all_gather.15 = bf16[16,32,16]{1,2,0:T(8,128)(2,1)S(1)} all-gather(bf16[8,32,16]{1,2,0:T(8,128)(2,1)S(1)} %fusion.41), channel_id=1, replica_groups=mesh['groups'=1,'res'=16,'sub'=2] {'sub'}, dimensions={0}, use_global_device_ids=true | all-gather | bytes 24576 | tf_op jit(solution)/shard_map/all_gather | solution.py:45
  22.2 22.4 %all-gather.1 = bf16[16,256]{0,1:T(8,128)(2,1)S(1)} all-gather(bf16[16,16]{0,1:T(8,128)(2,1)S(1)} %copy.51), channel_id=3, replica_groups=mesh['groups'=1,'res'=16,'sub'=2] {'res'}, dimensions={1}, use_global_device_ids=true | all-gather | bytes 8704 | tf_op jit(solution)/shard_map/all_gather | solution.py:50
  44.6 20.5 %all_gather.16 = bf16[16,32,256]{1,0,2:T(8,128)(2,1)S(1)} all-gather(bf16[16,32,16]{1,0,2:T(8,128)(2,1)S(1)} %copy.47), channel_id=1, replica_groups=mesh['groups'=1,'res'=16,'sub'=2] {'res'}, dimensions={2}, use_global_device_ids=true | all-gather | bytes 278528 | tf_op jit(solution)/shard_map/all_gather | solution.py:49
  65.1 0.2 fusion.42
  65.3 0.1 constant_dynamic-slice_fusion
  65.3 0.4 copy.65
  65.8 0.0 copy-start.8
  65.8 1.3 convolution_bitcast_fusion
  67.1 1.9 copy-done.1
  69.0 4.9 %fusion.35 = f32[16,32,16]{1,2,0:T(8,128)} fusion(f32[16,16,32,128]{3,2,1,0:T(8,128)S(1)} %convolution_bitcast_fusion, bf16[32,32,128]{2,1,0:T(8,128)(2,1)S(1)} %bitcast.85), kind=kOutput, calls=%fused_computation.19 | convolution fusion | flops 402653184 | bytes 4489216 | tf_op jit(solution)/shard_map/side,cde->sci/dot_general | solution.py:71
  74.0 0.0 reduce-scatter.4.cloned.1.call-update
  74.0 0.0 reduce-scatter.6.cloned.1.call-start
  74.0 0.2 fusion.40
  74.3 4.6 %all_gather.17 = bf16[16,32,16]{1,2,0:T(8,128)(2,1)S(1)} all-gather(bf16[8,32,16]{1,2,0:T(8,128)(2,1)S(1)} %fusion.40), channel_id=1, replica_groups=mesh['groups'=1,'res'=16,'sub'=2] {'sub'}, dimensions={0}, use_global_device_ids=true | all-gather | bytes 24576 | tf_op jit(solution)/shard_map/all_gather | solution.py:44
  78.9 0.7 convolution_convert_fusion
  79.6 0.2 broadcast_in_dim.2
  79.8 1.1 copy-done.4
  80.9 1.9 fusion.14
  82.8 1.3 copy-done.2
  84.1 0.0 reduce-scatter.6.cloned.1.call-update
  84.2 0.2 all-reduce.3.cloned.1.call-start
  84.4 6.8 %fusion.26 = f32[32,32,128]{2,0,1:T(8,128)} fusion(f32[16,16,32,128]{3,2,1,0:T(8,128)} %copy-done.1, bf16[16,32,16]{1,2,0:T(8,128)(2,1)S(1)} %all_gather.17), kind=kOutput, calls=%fused_computation.16 | convolution fusion | flops 402653184 | bytes 4734976 | tf_op jit(solution)/shard_map/sci,side->cde/dot_general | solution.py:72
  91.3 0.0 all-reduce.3.cloned.1.call-update
  91.3 0.0 reduce-scatter.8.cloned.1.call-start
  91.3 0.6 fusion.45
  92.0 2.3 fusion.32
  94.3 1.1 convolution_bitcast_fusion.2
  95.5 1.1 fusion.67
  96.5 52.7 %reduce-scatter.6.cloned.1.call-done = f32[16,32,16]{1,2,0:T(8,128)} async-done(((f32[16,32,256]{1,2,0:T(8,128)}), f32[16,32,16]{1,2,0:T(8,128)}) %reduce-scatter.6.cloned.1.call-update) | async-done | bytes 32784 | tf_op jit(solution)/shard_map/reduce_scatter | solution.py:75
  149.2 0.0 reduce-scatter.8.cloned.1.call-update
  149.3 71.2 %all-reduce.3.cloned.1.call-done = f32[32,32,128]{2,0,1:T(8,128)} async-done(((f32[32,32,128]{2,0,1:T(8,128)}), f32[32,32,128]{2,0,1:T(8,128)}) %all-reduce.3.cloned.1.call-update) | async-done | bytes 524304 | tf_op jit(solution)/shard_map/psum | solution.py:85
  220.5 1.1 broadcast_multiply_fusion
  221.5 1.1 copy.57
  222.7 1.1 convolution_bitcast_fusion.1
  223.8 39.6 %all-reduce = (f32[64,32]{0,1:T(8,128)S(1)}, f32[64,32]{0,1:T(8,128)S(1)}, f32[128]{0:T(128)S(1)}) all-reduce(f32[64,32]{0,1:T(8,128)S(1)} %convolution_bitcast_fusion.2, f32[64,32]{0,1:T(8,128)S(1)} %convolution_bitcast_fusion.1, f32[128]{0:T(128)S(1)} %fusion.45), channel_id=1, replica_groups=mesh['groups'=1,'res'=16,'sub'=2] {'res','sub'}, use_global_device_ids=true, to_apply=%region_7.0 | all-reduce | flops 4224 | bytes 33792 | tf_op jit(solution)/shard_map/psum | solution.py:85
  263.4 0.5 broadcast_multiply_fusion.6
  263.9 0.6 broadcast_multiply_fusion.1
  264.5 1.2 fusion.85
  265.7 0.8 fusion.60
  (25 shorter events, 0.1 us)
Async XLA Ops:
  8.0 8.7 %copy-start = (bf16[64,32]{0,1:T(8,128)(2,1)S(1)}, bf16[64,32]{0,1:T(8,128)(2,1)}, u32[]{:S(2)}) copy-start(bf16[64,32]{0,1:T(8,128)(2,1)} %param.12) | copy-start | bytes 12292
  8.0 57.8 %copy-start.3 = (f32[16,128,128]{2,1,0:T(8,128)S(1)}, f32[16,128,128]{2,1,0:T(8,128)}, u32[]{:S(2)}) copy-start(f32[16,128,128]{2,1,0:T(8,128)} %param.15) | copy-start | bytes 3145732
  8.0 86.3 %reduce-scatter.4.cloned.1.call-start = ((), (), s32[]{:S(2)}) async-start(), calls=%async_computation.3 | async-start | bytes 196608 | tf_op jit(solution)/shard_map/reduce_scatter | solution.py:77
  65.8 1.3 copy-start.8
  65.8 3.2 %copy-start.6 = (bf16[1024,128]{1,0:T(8,128)(2,1)S(1)}, bf16[1024,128]{1,0:T(8,128)(2,1)}, u32[]{:S(2)}) copy-start(bf16[1024,128]{1,0:T(8,128)(2,1)} %param.13) | copy-start | bytes 786436
  67.1 1.9 copy-start.1
  69.0 5.0 %copy-start.7 = (bf16[8,16,64]{2,1,0:T(8,128)(2,1)S(1)}, bf16[8,16,64]{2,1,0:T(8,128)(2,1)}, u32[]{:S(2)}) copy-start(bf16[8,16,64]{2,1,0:T(8,128)(2,1)} %param.8) | copy-start | bytes 49156
  69.0 5.0 %copy-start.10 = (bf16[64,32]{0,1:T(8,128)(2,1)S(1)}, bf16[64,32]{0,1:T(8,128)(2,1)}, u32[]{:S(2)}) copy-start(bf16[64,32]{0,1:T(8,128)(2,1)} %param.11) | copy-start | bytes 12292
  74.0 75.3 %reduce-scatter.6.cloned.1.call-start = ((), (), s32[]{:S(2)}) async-start(), calls=%async_computation.4 | async-start | bytes 2228224 | tf_op jit(solution)/shard_map/reduce_scatter | solution.py:75
  79.6 1.3 copy-start.4
  82.8 1.3 copy-start.2
  84.2 7.8 %copy-start.5 = (bf16[16,16,32,128]{3,1,2,0:T(8,128)(2,1)S(1)}, bf16[16,16,32,128]{3,1,2,0:T(8,128)(2,1)}, u32[]{:S(2)}) copy-start(bf16[16,16,32,128]{3,1,2,0:T(8,128)(2,1)} %copy-done.4) | copy-start | bytes 6291460
  84.2 7.8 %copy-start.9 = (bf16[16,32,128]{2,1,0:T(8,128)(2,1)S(1)}, bf16[16,32,128]{2,1,0:T(8,128)(2,1)}, u32[]{:S(2)}) copy-start(bf16[16,32,128]{2,1,0:T(8,128)(2,1)} %copy-done.8) | copy-start | bytes 393220
  84.2 7.8 %copy-start.11 = (f32[128]{0:T(128)S(1)}, f32[128]{0:T(128)}, u32[]{:S(2)}) copy-start(f32[128]{0:T(128)} %param.14) | copy-start | bytes 1540
  84.2 136.3 %all-reduce.3.cloned.1.call-start = ((), (), s32[]{:S(2)}) async-start(), calls=%async_computation.6 | async-start | bytes 1048576 | tf_op jit(solution)/shard_map/psum | solution.py:85
  91.3 131.4 %reduce-scatter.8.cloned.1.call-start = ((), (), s32[]{:S(2)}) async-start(), calls=%async_computation.5 | async-start | bytes 196608 | tf_op jit(solution)/shard_map/reduce_scatter | solution.py:78
Sparse Core Ops, SparseCore 0:
  74.1 9.7 reduce-scatter.3
  87.6 61.6 reduce-scatter.5
  151.5 9.2 reduce-scatter.7
Sparse Core Ops, SparseCore 1:
  91.4 129.0 all-reduce.2
where the time goes:
time: 274 us
  waiting for transfers between devices  124 us (45%)
  blocking collectives  96.9 us (35%)
  matrix products  23.8 us (9%)
  between operations  15.5 us (6%)
  other arithmetic  6.85 us (2%)
  local copies, waits for them, and re-layouts  6.32 us (2%)
    psum x1, waiting for transfers between devices, body(): totals = lax.psum((out_part, bias_part, wa_part, wb_part), ('res', 'sub'))  71.2 us
    reduce_scatter x1, waiting for transfers between devices, body(): lax.psum_scatter(placed, 'res', scatter_dimension=2, tiled=True)  52.7 us
    psum x1, blocking collectives, body(): totals = lax.psum((out_part, bias_part, wa_part, wb_part), ('res', 'sub'))  39.6 us
    all_gather x1, blocking collectives, body(): lax.all_gather(all_mask, 'res', axis=2, tiled=True)  22.4 us
    all_gather x1, blocking collectives, body(): lax.all_gather(all_b, 'res', axis=2, tiled=True)  20.5 us
    dot_general x1, matrix products, body(): jnp.einsum('sci,side->cde', all_a.astype(precise_scalar), dtmix, precisio...  6.84 us
  transfers between devices with their start and end apart: 4, of which 2 were waited for; matrix products, arithmetic and copies ran while one was open for 6% of the time, Pallas kernels for 0%

commit v1 on v0

--- a/solution.py
+++ b/solution.py
@@ -1,7 +1,411 @@
+import functools
+
 import jax
 import jax.numpy as jnp
 from jax import lax
 from jax.sharding import PartitionSpec as P
+from jax.experimental import pallas as pl
+from jax.experimental.pallas import tpu as pltpu
+
+
+MESH = pl.DeviceIdType.MESH
+
+
+def onehot(shape, test):
+    rows = lax.broadcasted_iota(jnp.int32, shape, 0)
+    lanes = lax.broadcasted_iota(jnp.int32, shape, 1)
+    return jnp.where(test(rows, lanes), 1.0, 0.0)
+
+
+def dot(a, b, dims=((1,), (0,)), precision=None):
+    return lax.dot_general(a, b, (dims, ((), ())), preferred_element_type=jnp.float32, precision=precision)
+
+
+def kernel(
+    nres, nsub,
+    emb, flags, pflags, wab, lin, offset, cot_hbm,
+    pair, align, wa_out, wb_out, lin_out, bias_out,
+    cot, feat, other, blk, bmat, wm, lin32, tmat, gmat, dmat, wide, dstage, drecv,
+    ostage, orecv, ogather, da_send, da_recv, small, small_recv, rows_out,
+    cot_sem, bsend, brecv, dsend, drecv_sem, osend, orecv_sem, gsend, grecv, wsend, wrecv, psend, precv,
+):
+    bf16, f32 = jnp.bfloat16, jnp.float32
+    n = nres * nsub
+    nblk = nres // nsub
+    r, u = lax.axis_index("res"), lax.axis_index("sub")
+    me = r * nsub + u
+
+    def place(k):
+        return {"res": k // nsub, "sub": lax.rem(k, nsub)}
+
+    cot_copy = pltpu.make_async_copy(cot_hbm, cot, cot_sem)
+    cot_copy.start()
+    barrier = pltpu.get_barrier_semaphore()
+
+    def greet(k, carry):
+        pl.semaphore_signal(barrier, inc=1, device_id=place(lax.rem(me + k, n)), device_id_type=MESH)
+        return carry
+
+    lax.fori_loop(1, n, greet, 0)
+
+    x = dot(onehot((128, 128), lambda a, b: b == (a % 8) * 16 + a // 8).astype(bf16), emb[...].reshape(128, 64))
+    centred = x - jnp.mean(x, axis=-1, keepdims=True)
+    inv_std = lax.rsqrt(jnp.mean(centred * centred, axis=-1, keepdims=True) + 1e-05)
+    normed = centred * inv_std
+    normed16 = normed.astype(bf16)
+    picked = dot(onehot((128, 8), lambda a, b: a % 8 == b).astype(bf16), flags[...].astype(f32).astype(bf16))
+    mask = jnp.sum(picked * onehot((128, 16), lambda a, b: a // 8 == b), axis=1, keepdims=True)
+    projected = dot(normed16, wab[...]) * mask
+    projected = projected + mask * onehot((128, 128), lambda a, b: b - 64 == a % 8)
+    feat[...] = projected.astype(bf16)
+    keep = onehot((128, 384), lambda a, b: a % 8 == b % 8)
+    spread = onehot((128, 384), lambda a, b: ((b < 256) & (a == 32 + b // 8)) | ((a >= 64) & (b - 256 == a)))
+    gather_rows = onehot((16, 128), lambda a, b: a == b // 8).astype(bf16)
+    mine = dot(gather_rows, (dot(feat[...], spread.astype(bf16)) * keep).astype(bf16)).astype(bf16)
+    blk[...] = mine
+    home = r // nblk
+    slot = u * nblk + lax.rem(r, nblk)
+    rows_here = pl.ds(pl.multiple_of(lax.rem(r, nblk) * 16, 16), 16)
+
+    pl.semaphore_wait(barrier, n - 1)
+
+    def partner_copy():
+        return pltpu.make_async_remote_copy(
+            src_ref=feat, dst_ref=other, send_sem=psend.at[0], recv_sem=precv.at[0],
+            device_id={"res": r, "sub": 1 - u}, device_id_type=MESH)
+
+    partner_copy().start()
+
+    def block_copy(k):
+        q = lax.rem(r + k, nres)
+        return pltpu.make_async_remote_copy(
+            src_ref=blk, dst_ref=bmat.at[u, rows_here, :], send_sem=bsend.at[k], recv_sem=brecv.at[slot],
+            device_id={"res": q, "sub": home}, device_id_type=MESH)
+
+    def send_block(k, carry):
+        block_copy(k).start()
+        return carry
+
+    lax.fori_loop(1, nres, send_block, 0)
+
+    @pl.when(home != u)
+    def _():
+        block_copy(0).start()
+
+    @pl.when(home == u)
+    def _():
+        bmat[u, rows_here, :] = mine
+
+    lin32[...] = lin[...].astype(f32)
+    wm[...] = jnp.zeros_like(wm)
+    for d in range(32):
+        piece = lin32[pl.ds(d, 32, stride=32), :].astype(bf16)
+        wm[0:32, d * 128:(d + 1) * 128] = piece
+        wm[64:96, d * 128:(d + 1) * 128] = piece
+
+    lane128 = lax.broadcasted_iota(jnp.int32, (128, 128), 1)
+
+    def left_only(ref):
+        return jnp.where(lane128 < 32, ref[...].astype(f32), 0.0)
+
+    def mix(half, left):
+        def step(p, carry):
+            part = dot(left, wm[:, pl.ds(pl.multiple_of(p * 256, 256), 256)])
+            for i in range(16):
+                rows = part[i * 8:(i + 1) * 8, :]
+                pair_rows = jnp.concatenate([rows[:, :128], rows[:, 128:]], axis=0)
+                tmat[half, pl.ds(pl.multiple_of(p * 16, 16), 16), i * 128:(i + 1) * 128] = pair_rows.astype(bf16)
+            return carry
+
+        lax.fori_loop(0, 16, step, 0)
+
+    mine_left = left_only(feat)
+    mix(u, mine_left.astype(bf16))
+    partner_copy().wait()
+    other_left = left_only(other)
+    mix(1 - u, other_left.astype(bf16))
+
+    mask_rows = [dot(gather_rows, ref[...]).astype(bf16) for ref in (feat, other)]
+
+    cot_copy.wait()
+
+    def wait_block(k, carry):
+        @pl.when(k != slot)
+        def _():
+            copy = pltpu.make_async_remote_copy(
+                src_ref=blk, dst_ref=bmat.at[k // nblk, pl.ds(pl.multiple_of(lax.rem(k, nblk) * 16, 16), 16), :],
+                send_sem=bsend.at[0], recv_sem=brecv.at[k], device_id={"res": r, "sub": 1 - u}, device_id_type=MESH)
+            copy.wait_recv()
+
+        @pl.when((k == slot) & (home != u))
+        def _():
+            copy = pltpu.make_async_remote_copy(
+                src_ref=blk, dst_ref=bmat.at[k // nblk, pl.ds(pl.multiple_of(lax.rem(k, nblk) * 16, 16), 16), :],
+                send_sem=bsend.at[0], recv_sem=brecv.at[k], device_id={"res": r, "sub": 1 - u}, device_id_type=MESH)
+            copy.wait_recv()
+
+        return carry
+
+    lax.fori_loop(0, nres, wait_block, 0)
+
+    count = dot(mask_rows[0], bmat[u, :, 256:384], ((1,), (1,))) + dot(mask_rows[1], bmat[1 - u, :, 256:384], ((1,), (1,)))
+    scale = (pflags[...].astype(f32) / jnp.maximum(count, 1.0)).T
+    bias = jnp.zeros((1, 128), f32)
+    for i in range(16):
+        g32 = cot[i] * scale[:, i:i + 1]
+        bias = bias + jnp.sum(g32, axis=0, keepdims=True)
+        gmat[:, i * 128:(i + 1) * 128] = g32.astype(bf16)
+
+    for half in range(2):
+        db = dot(gmat[...], tmat[half], ((1,), (1,))).astype(bf16)
+        for k in range(nblk):
+            dstage[k * 2 + half] = db[k * 16:(k + 1) * 16, :]
+
+    def grad_copy(k, t):
+        return pltpu.make_async_remote_copy(
+            src_ref=dstage.at[t], dst_ref=drecv.at[r], send_sem=dsend.at[t], recv_sem=drecv_sem.at[k],
+            device_id={"res": u * nblk + t // nsub, "sub": lax.rem(t, nsub)}, device_id_type=MESH)
+
+    def is_self(t):
+        return (u * nblk + t // nsub == r) & (lax.rem(t, nsub) == u)
+
+    def send_grad(k, carry):
+        t = lax.rem(k + me, nres)
+
+        @pl.when(jnp.logical_not(is_self(t)))
+        def _():
+            grad_copy(r, t).start()
+
+        @pl.when(is_self(t))
+        def _():
+            drecv[r] = dstage[t]
+
+        return carry
+
+    lax.fori_loop(0, nres, send_grad, 0)
+
+    bt = [bmat[half, :, 0:256].astype(f32).T.astype(bf16) for half in range(2)]
+
+    def back(p, carry):
+        g = gmat[:, pl.ds(pl.multiple_of(p * 256, 256), 256)]
+        for half in range(2):
+            part = dot(bt[half], g)
+            for d in range(32):
+                rows = part[d * 8:(d + 1) * 8, :]
+                pair_rows = jnp.concatenate([rows[:, :128], rows[:, 128:]], axis=0)
+                dmat[half, pl.ds(pl.multiple_of(p * 16, 16), 16), d * 128:(d + 1) * 128] = pair_rows.astype(bf16)
+        return carry
+
+    lax.fori_loop(0, 8, back, 0)
+
+    at_mine = mine_left.T[0:32].astype(bf16)
+    at_other = other_left.T[0:32].astype(bf16)
+    for q in range(8):
+        lanes = slice(q * 512, (q + 1) * 512)
+        part = dot(at_mine, dmat[u, :, lanes]) + dot(at_other, dmat[1 - u, :, lanes])
+        for k in range(4):
+            ostage[q * 4 + k] = part[:, k * 128:(k + 1) * 128].astype(bf16)
+
+    def weight_copy(dst, src):
+        return pltpu.make_async_remote_copy(
+            src_ref=ostage.at[dst], dst_ref=orecv.at[src], send_sem=osend.at[dst], recv_sem=orecv_sem.at[src],
+            device_id=place(dst), device_id_type=MESH)
+
+    def send_weight(k, carry):
+        weight_copy(lax.rem(me + k, n), me).start()
+        return carry
+
+    lax.fori_loop(1, n, send_weight, 0)
+    orecv[me] = ostage[me]
+
+    da_send[...] = dot(dmat[1 - u], wm[...], ((1,), (1,)))
+
+    def da_copy():
+        return pltpu.make_async_remote_copy(
+            src_ref=da_send, dst_ref=da_recv, send_sem=psend.at[1], recv_sem=precv.at[1],
+            device_id={"res": r, "sub": 1 - u}, device_id_type=MESH)
+
+    da_copy().start()
+    da = dot(dmat[u], wm[...], ((1,), (1,)))
+
+    for p in range(8):
+        lanes = slice(p * 256, (p + 1) * 256)
+        z = dot(bmat[0, :, 0:256], tmat[0, :, lanes]) + dot(bmat[1, :, 0:256], tmat[1, :, lanes])
+        for k in range(2):
+            i = p * 2 + k
+            pair[i] = ((z[:, k * 128:(k + 1) * 128] + offset[...]) * scale[:, i:i + 1]).astype(bf16)
+
+    da_copy().wait()
+
+    def wait_grad(k, carry):
+        @pl.when((k != r) | (home != u))
+        def _():
+            grad_copy(k, 0).wait_recv()
+
+        return carry
+
+    lax.fori_loop(0, nres, wait_grad, 0)
+    total = drecv[0].astype(f32)
+    for k in range(1, nres):
+        total = total + drecv[k].astype(f32)
+    highest = lax.Precision.HIGHEST
+    wide_rows = dot(onehot((128, 16), lambda a, b: a // 8 == b), total, precision=highest) * keep[:, :256]
+    db_rows = dot(wide_rows, onehot((256, 128), lambda a, b: b % 64 == 32 + a // 8), precision=highest)
+    dfeat = ((da + da_recv[...] + db_rows) * mask).astype(bf16)
+    grads = dot(normed16, dfeat, ((0,), (0,)))
+    low = lax.broadcasted_iota(jnp.int32, (32, 128), 1) < 64
+    small[0:32] = jnp.where(low, grads[0:32], grads[32:64]).astype(bf16)
+    small[32:48] = jnp.broadcast_to(bias, (16, 128)).astype(bf16)
+
+    def small_copy(dst, src):
+        return pltpu.make_async_remote_copy(
+            src_ref=small, dst_ref=small_recv.at[src], send_sem=wsend.at[dst], recv_sem=wrecv.at[src],
+            device_id=place(dst), device_id_type=MESH)
+
+    def send_small(k, carry):
+        small_copy(lax.rem(me + k, n), me).start()
+        return carry
+
+    lax.fori_loop(1, n, send_small, 0)
+    small_recv[me] = small[...]
+
+    def wait_weight(k, carry):
+        weight_copy(0, lax.rem(me + k, n)).wait_recv()
+        return carry
+
+    lax.fori_loop(1, n, wait_weight, 0)
+    owned = lax.fori_loop(1, n, lambda k, t: t + orecv[k].astype(f32), orecv[0].astype(f32))
+    ogather[me] = owned.astype(bf16)
+
+    def gather_copy(dst, src):
+        return pltpu.make_async_remote_copy(
+            src_ref=ogather.at[me], dst_ref=ogather.at[src], send_sem=gsend.at[dst], recv_sem=grecv.at[src],
+            device_id=place(dst), device_id_type=MESH)
+
+    def send_gather(k, carry):
+        gather_copy(lax.rem(me + k, n), me).start()
+        return carry
+
+    lax.fori_loop(1, n, send_gather, 0)
+
+    dnormed = dot(dfeat, wab[...], ((1,), (1,)))
+    rows_out[...] = inv_std * (
+        dnormed - jnp.mean(dnormed, axis=-1, keepdims=True)
+        - normed * jnp.mean(dnormed * normed, axis=-1, keepdims=True))
+    for s in range(8):
+        align[s] = rows_out[pl.ds(s, 16, stride=8), :]
+
+    def wait_small(k, carry):
+        small_copy(0, lax.rem(me + k, n)).wait_recv()
+        return carry
+
+    lax.fori_loop(1, n, wait_small, 0)
+    inv = 1.0 / (16 * nres)
+    sums = lax.fori_loop(1, n, lambda k, t: t + small_recv[k].astype(f32), small_recv[0].astype(f32)) * inv
+    wa_out[0:32] = sums[0:32, 0:32]
+    wa_out[32:64] = sums[0:32, 64:96]
+    wb_out[0:32] = sums[0:32, 32:64]
+    wb_out[32:64] = sums[0:32, 96:128]
+    bias_out[...] = sums[32:33]
+
+    def wait_gather(k, carry):
+        gather_copy(0, lax.rem(me + k, n)).wait_recv()
+        return carry
+
+    lax.fori_loop(1, n, wait_gather, 0)
+    for d in range(32):
+        lin_out[pl.ds(d, 32, stride=32), :] = ogather[d].astype(f32) * inv
+
+    def drain(k, carry):
+        dst = lax.rem(me + k, n)
+        weight_copy(dst, me).wait_send()
+        small_copy(dst, me).wait_send()
+        gather_copy(dst, me).wait_send()
+        return carry
+
+    lax.fori_loop(1, n, drain, 0)
+
+    def drain_near(k, carry):
+        @pl.when((k != 0) | (home != u))
+        def _():
+            block_copy(k).wait_send()
+
+        @pl.when(jnp.logical_not(is_self(k)))
+        def _():
+            grad_copy(r, k).wait_send()
+
+        return carry
+
+    lax.fori_loop(0, nres, drain_near, 0)
+
+
+def fused(
+    nres, nsub,
+    sequence_embedding,
+    sequence_present_flags,
+    position_couple_flags,
+    first_factor_matrix,
+    second_factor_matrix,
+    final_linear_matrix,
+    final_offset_vector,
+    couple_change_cotangent,
+):
+    bf16, f32 = jnp.bfloat16, jnp.float32
+    n = nres * nsub
+    zeros = jnp.zeros((64, 64), bf16)
+    wab = jnp.concatenate([first_factor_matrix, second_factor_matrix, zeros], axis=1)
+    vmem = pl.BlockSpec(memory_space=pltpu.VMEM)
+    dma = pltpu.SemaphoreType.DMA
+    outs = pl.pallas_call(
+        functools.partial(kernel, nres, nsub),
+        out_shape=(
+            jax.ShapeDtypeStruct((16, 128, 128), bf16),
+            jax.ShapeDtypeStruct((8, 16, 64), f32),
+            jax.ShapeDtypeStruct((64, 32), f32),
+            jax.ShapeDtypeStruct((64, 32), f32),
+            jax.ShapeDtypeStruct((1024, 128), f32),
+            jax.ShapeDtypeStruct((1, 128), f32),
+        ),
+        in_specs=[vmem] * 6 + [pl.BlockSpec(memory_space=pl.ANY)],
+        out_specs=(vmem,) * 6,
+        scratch_shapes=[
+            pltpu.VMEM((16, 128, 128), f32),
+            pltpu.VMEM((128, 128), bf16),
+            pltpu.VMEM((128, 128), bf16),
+            pltpu.VMEM((16, 384), bf16),
+            pltpu.VMEM((2, 128, 384), bf16),
+            pltpu.VMEM((128, 4096), bf16),
+            pltpu.VMEM((1024, 128), f32),
+            pltpu.VMEM((2, 256, 2048), bf16),
+            pltpu.VMEM((128, 2048), bf16),
+            pltpu.VMEM((2, 128, 4096), bf16),
+            pltpu.VMEM((8, 128), f32),
+            pltpu.VMEM((nres, 16, 256), bf16),
+            pltpu.VMEM((nres, 16, 256), bf16),
+            pltpu.VMEM((n, 32, 128), bf16),
+            pltpu.VMEM((n, 32, 128), bf16),
+            pltpu.VMEM((n, 32, 128), bf16),
+            pltpu.VMEM((128, 128), f32),
+            pltpu.VMEM((128, 128), f32),
+            pltpu.VMEM((48, 128), bf16),
+            pltpu.VMEM((n, 48, 128), bf16),
+            pltpu.VMEM((128, 64), f32),
+            dma,
+            dma((nres,)), dma((nres,)),
+            dma((nres,)), dma((nres,)),
+            dma((n,)), dma((n,)),
+            dma((n,)), dma((n,)),
+            dma((n,)), dma((n,)),
+            dma((2,)), dma((2,)),
+        ],
+        compiler_params=pltpu.CompilerParams(
+            collective_id=0, has_side_effects=True, vmem_limit_bytes=48 * 1024 * 1024
+        ),
+    )(
+        sequence_embedding, sequence_present_flags, position_couple_flags, wab,
+        final_linear_matrix, final_offset_vector.reshape(1, 128), couple_change_cotangent,
+    )
+    return (*outs[:5], outs[5].reshape(128))
 
 
 def body(
@@ -129,4 +533,6 @@
         P("groups", None),
         P("groups"),
     )
-    return jax.shard_map(body, mesh=mesh, in_specs=in_specs, out_specs=out_specs, check_vma=False)
+    nres, nsub = mesh.shape["res"], mesh.shape["sub"]
+    chosen = functools.partial(fused, nres, nsub) if (nres, nsub) == (16, 2) else body
+    return jax.shard_map(chosen, mesh=mesh, in_specs=in_specs, out_specs=out_specs, check_vma=False)

time: 274 us -> 52.6 us (0.19)
  waiting for transfers between devices: 124 us -> 0 us
  blocking collectives: 96.9 us -> 0 us
  Pallas kernels: 0 us -> 43.7 us
  matrix products: 23.8 us -> 0 us
  between operations: 15.5 us -> 0.69 us
  other arithmetic: 6.85 us -> 0.08 us
    psum x1 -> x0, waiting for transfers between devices: 71.2 us -> none  [body(): totals = lax.psum((out_part, bias_part, wa_part, wb_part), ('res', 'sub'))]
    all_gather x5 -> x0, blocking collectives: 57.3 us -> none  [the longest x1 22.4 us: body(): lax.all_gather(all_mask, 'res', axis=2, tiled=True)]
    reduce_scatter x3 -> x0, waiting for transfers between devices: 52.7 us -> none  [the longest x1 52.7 us: body(): lax.psum_scatter(placed, 'res', scatter_dimension=2, tiled=True)]
    pallas_call x0 -> x1, Pallas kernels: none -> 43.7 us  [fused(): pl.pallas_call(functools.partial(kernel, nres, nsub), out_shape=(jax.Shap...]
    psum x1 -> x0, blocking collectives: 39.6 us -> none  [body(): totals = lax.psum((out_part, bias_part, wa_part, wb_part), ('res', 'sub'))]
    dot_general x13 -> x0, matrix products: 23.8 us -> none  [the longest x1 6.84 us: body(): jnp.einsum('sci,side->cde', all_a.astype(precise_scalar), dtmix, precisio...]
    mul x4 -> x0, other arithmetic: 2.97 us -> none  [the longest x1 1.08 us: body(): totals[0].reshape(hidden * hidden, pair_width) * inv_res]
    unnamed x25 -> x22, local copies, waits for them, and re-layouts: 4.88 us -> 7.77 us
  transfers between devices with their start and end apart: 4 -> 0, of which waited for: 2 -> 0; matrix products, arithmetic and copies ran while one was open for 6% -> 0% of each run, Pallas kernels for 0% -> 0%
where the time goes in v1:
time: 52.6 us; the launch traced here: 52.3 us
  Pallas kernels  43.7 us (83%)
  local copies, waits for them, and re-layouts  7.85 us (15%)
  between operations  0.69 us (1%)
    pallas_call x1, Pallas kernels, fused(): pl.pallas_call(functools.partial(kernel, nres, nsub), out_shape=(jax.Shap...  43.7 us
    unnamed x22, local copies, waits for them, and re-layouts  7.77 us

profile of v1, /device:TPU:0, one launch (start us, length us, event | category | flops | bytes accessed | tf_op | source)
XLA Modules:
  0.0 52.3 jit_solution(9413784240946161627)
XLA Ops:
  0.6 0.1 pad.2.clone
  0.7 0.0 copy-start.6
  0.7 0.8 %copy.14 = bf16[64,32]{1,0:T(8,128)(2,1)S(1)} copy(bf16[64,32]{0,1:T(8,128)(2,1)} %param.11) | data formatting | bytes 8192 | tf_op args[3]
  1.5 0.0 copy-done.6
  1.5 0.0 copy-start.2
  1.5 0.1 copy.15
  1.6 0.0 copy-start.3
  1.6 0.0 copy-start.4
  1.7 0.0 copy-start.5
  1.7 0.1 maximum_maximum_fusion.wab
  1.7 0.5 %copy-done.2 = bf16[8,16,64]{2,1,0:T(8,128)(2,1)S(1)} copy-done((bf16[8,16,64]{2,1,0:T(8,128)(2,1)S(1)}, bf16[8,16,64]{2,1,0:T(8,128)(2,1)}, u32[]{:S(2)}) %copy-start.2) | copy-done | bytes 16408
  2.3 0.1 copy-done.3
  2.3 0.0 copy-done.4
  2.3 0.0 copy-done.5
  2.4 0.0 copy-start
  2.4 1.2 %copy-done = f32[16,128,128]{2,1,0:T(8,128)S(1)} copy-done((f32[16,128,128]{2,1,0:T(8,128)S(1)}, f32[16,128,128]{2,1,0:T(8,128)}, u32[]{:S(2)}) %copy-start) | copy-done | bytes 1048600
  3.6 0.0 copy-start.1
  3.6 0.9 %copy-done.1 = bf16[1024,128]{1,0:T(8,128)(2,1)S(1)} copy-done((bf16[1024,128]{1,0:T(8,128)(2,1)S(1)}, bf16[1024,128]{1,0:T(8,128)(2,1)}, u32[]{:S(2)}) %copy-start.1) | copy-done | bytes 262168
  4.5 43.7 %shard_map.127 = (bf16[16,128,128]{2,1,0:T(8,128)(2,1)S(1)}, f32[8,16,64]{2,1,0:T(8,128)S(1)}, f32[64,32]{1,0:T(8,128)S(1)}, f32[64,32]{1,0:T(8,128)S(1)}, f32[1...) custom-call(bf16[8,16,64]{2,1,0:T(8,128)(2,1)S(1)} %copy-done.2, s32[8,16]{1,0:T(8,128)S(1)} %copy-done.4, ...), custom_call_target="tpu_custom_call" | custom-call | tf_op jit(solution)/shard_map/pallas_call | solution.py:359
  48.2 0.7 %copy.16 = f32[64,32]{0,1:T(8,128)} copy(f32[64,32]{1,0:T(8,128)S(1)} %get-tuple-element.20) | data formatting | bytes 16384
  48.9 0.7 %copy.17 = f32[64,32]{0,1:T(8,128)} copy(f32[64,32]{1,0:T(8,128)S(1)} %get-tuple-element.21) | data formatting | bytes 16384
  49.6 0.8 %copy.22 = bf16[16,128,128]{2,1,0:T(8,128)(2,1)} copy(bf16[16,128,128]{2,1,0:T(8,128)(2,1)S(1)} %get-tuple-element.30) | data formatting | bytes 1048576
  50.4 0.6 %copy.23 = f32[8,16,64]{2,1,0:T(8,128)} copy(f32[8,16,64]{2,1,0:T(8,128)S(1)} %get-tuple-element.31) | data formatting | bytes 65536
  51.0 0.8 %copy.24 = f32[1024,128]{1,0:T(8,128)} copy(f32[1024,128]{1,0:T(8,128)S(1)} %get-tuple-element.34) | data formatting | bytes 1048576
  51.8 0.5 copy.25
  (1 shorter events, 0.0 us)
Async XLA Ops:
  0.7 0.8 %copy-start.6 = (bf16[64,32]{0,1:T(8,128)(2,1)S(1)}, bf16[64,32]{0,1:T(8,128)(2,1)}, u32[]{:S(2)}) copy-start(bf16[64,32]{0,1:T(8,128)(2,1)} %param.12) | copy-start | bytes 12292
  1.5 0.8 %copy-start.2 = (bf16[8,16,64]{2,1,0:T(8,128)(2,1)S(1)}, bf16[8,16,64]{2,1,0:T(8,128)(2,1)}, u32[]{:S(2)}) copy-start(bf16[8,16,64]{2,1,0:T(8,128)(2,1)} %emb.1) | copy-start | bytes 49156
  1.6 0.7 %copy-start.3 = (s32[16,128]{1,0:T(8,128)S(1)}, s32[16,128]{1,0:T(8,128)}, u32[]{:S(2)}) copy-start(s32[16,128]{1,0:T(8,128)} %pflags.1) | copy-start | bytes 24580
  1.6 0.7 %copy-start.4 = (s32[8,16]{1,0:T(8,128)S(1)}, s32[8,16]{1,0:T(8,128)}, u32[]{:S(2)}) copy-start(s32[8,16]{1,0:T(8,128)} %flags.1) | copy-start | bytes 1540
  1.7 0.7 %copy-start.5 = (f32[128]{0:T(128)S(1)}, f32[128]{0:T(128)}, u32[]{:S(2)}) copy-start(f32[128]{0:T(128)} %param.14) | copy-start | bytes 1540
  2.4 1.2 %copy-start = (f32[16,128,128]{2,1,0:T(8,128)S(1)}, f32[16,128,128]{2,1,0:T(8,128)}, u32[]{:S(2)}) copy-start(f32[16,128,128]{2,1,0:T(8,128)} %cot_hbm.1) | copy-start | bytes 3145732
  3.6 0.9 %copy-start.1 = (bf16[1024,128]{1,0:T(8,128)(2,1)S(1)}, bf16[1024,128]{1,0:T(8,128)(2,1)}, u32[]{:S(2)}) copy-start(bf16[1024,128]{1,0:T(8,128)(2,1)} %lin.1) | copy-start | bytes 786436

commit v2 on v1

--- a/solution.py
+++ b/solution.py
@@ -23,11 +23,11 @@
 
 def kernel(
     nres, nsub,
-    emb, flags, pflags, wab, lin, offset, cot_hbm,
+    emb_hbm, flags_hbm, pflags_hbm, wa_hbm, wb_hbm, lin_hbm, offset_hbm, cot_hbm,
     pair, align, wa_out, wb_out, lin_out, bias_out,
-    cot, feat, other, blk, bmat, wm, lin32, tmat, gmat, dmat, wide, dstage, drecv,
-    ostage, orecv, ogather, da_send, da_recv, small, small_recv, rows_out,
-    cot_sem, bsend, brecv, dsend, drecv_sem, osend, orecv_sem, gsend, grecv, wsend, wrecv, psend, precv,
+    emb, flags, pflags, wa_t, wb_t, lin, offset, cot, feat, other, blk, bmat, wm, lin32, tmat, gmat, dmat, dstage, drecv,
+    ostage, orecv, ogather, da_send, da_recv, small, small_recv, plane, plane_recv, rows_out,
+    in_sem, bsend, brecv, dsend, drecv_sem, osend, orecv_sem, gsend, grecv, wsend, wrecv, psend, precv, vsend, vrecv,
 ):
     bf16, f32 = jnp.bfloat16, jnp.float32
     n = nres * nsub
@@ -38,8 +38,17 @@
     def place(k):
         return {"res": k // nsub, "sub": lax.rem(k, nsub)}
 
-    cot_copy = pltpu.make_async_copy(cot_hbm, cot, cot_sem)
-    cot_copy.start()
+    ins = [
+        pltpu.make_async_copy(a, b, in_sem.at[k])
+        for k, (a, b) in enumerate([
+            (emb_hbm, emb), (flags_hbm, flags), (wa_hbm, wa_t), (wb_hbm, wb_t),
+            (lin_hbm, lin), (pflags_hbm, pflags), (offset_hbm, offset), (cot_hbm, cot)])
+    ]
+    for copy in ins:
+        copy.start()
+    near = 8
+    far = n // near
+    spot, layer = lax.rem(me, near), me // near
     barrier = pltpu.get_barrier_semaphore()
 
     def greet(k, carry):
@@ -47,6 +56,10 @@
         return carry
 
     lax.fori_loop(1, n, greet, 0)
+
+    for copy in ins[:4]:
+        copy.wait()
+    wab_t = jnp.concatenate([wa_t[...], wb_t[...], jnp.zeros((64, 64), bf16)], axis=0)
 
     x = dot(onehot((128, 128), lambda a, b: b == (a % 8) * 16 + a // 8).astype(bf16), emb[...].reshape(128, 64))
     centred = x - jnp.mean(x, axis=-1, keepdims=True)
@@ -55,7 +68,7 @@
     normed16 = normed.astype(bf16)
     picked = dot(onehot((128, 8), lambda a, b: a % 8 == b).astype(bf16), flags[...].astype(f32).astype(bf16))
     mask = jnp.sum(picked * onehot((128, 16), lambda a, b: a // 8 == b), axis=1, keepdims=True)
-    projected = dot(normed16, wab[...]) * mask
+    projected = dot(normed16, wab_t, ((1,), (1,))) * mask
     projected = projected + mask * onehot((128, 128), lambda a, b: b - 64 == a % 8)
     feat[...] = projected.astype(bf16)
     keep = onehot((128, 384), lambda a, b: a % 8 == b % 8)
@@ -96,6 +109,7 @@
     def _():
         bmat[u, rows_here, :] = mine
 
+    ins[4].wait()
     lin32[...] = lin[...].astype(f32)
     wm[...] = jnp.zeros_like(wm)
     for d in range(32):
@@ -109,15 +123,12 @@
         return jnp.where(lane128 < 32, ref[...].astype(f32), 0.0)
 
     def mix(half, left):
-        def step(p, carry):
-            part = dot(left, wm[:, pl.ds(pl.multiple_of(p * 256, 256), 256)])
+        for p in range(16):
+            part = dot(left, wm[:, p * 256:(p + 1) * 256])
             for i in range(16):
                 rows = part[i * 8:(i + 1) * 8, :]
                 pair_rows = jnp.concatenate([rows[:, :128], rows[:, 128:]], axis=0)
-                tmat[half, pl.ds(pl.multiple_of(p * 16, 16), 16), i * 128:(i + 1) * 128] = pair_rows.astype(bf16)
-            return carry
-
-        lax.fori_loop(0, 16, step, 0)
+                tmat[half, p * 16:(p + 1) * 16, i * 128:(i + 1) * 128] = pair_rows.astype(bf16)
 
     mine_left = left_only(feat)
     mix(u, mine_left.astype(bf16))
@@ -127,7 +138,8 @@
 
     mask_rows = [dot(gather_rows, ref[...]).astype(bf16) for ref in (feat, other)]
 
-    cot_copy.wait()
+    for copy in ins[5:]:
+        copy.wait()
 
     def wait_block(k, carry):
         @pl.when(k != slot)
@@ -186,17 +198,14 @@
 
     bt = [bmat[half, :, 0:256].astype(f32).T.astype(bf16) for half in range(2)]
 
-    def back(p, carry):
-        g = gmat[:, pl.ds(pl.multiple_of(p * 256, 256), 256)]
+    for p in range(8):
+        g = gmat[:, p * 256:(p + 1) * 256]
         for half in range(2):
             part = dot(bt[half], g)
             for d in range(32):
                 rows = part[d * 8:(d + 1) * 8, :]
                 pair_rows = jnp.concatenate([rows[:, :128], rows[:, 128:]], axis=0)
-                dmat[half, pl.ds(pl.multiple_of(p * 16, 16), 16), d * 128:(d + 1) * 128] = pair_rows.astype(bf16)
-        return carry
-
-    lax.fori_loop(0, 8, back, 0)
+                dmat[half, p * 16:(p + 1) * 16, d * 128:(d + 1) * 128] = pair_rows.astype(bf16)
 
     at_mine = mine_left.T[0:32].astype(bf16)
     at_other = other_left.T[0:32].astype(bf16)
@@ -252,7 +261,8 @@
     wide_rows = dot(onehot((128, 16), lambda a, b: a // 8 == b), total, precision=highest) * keep[:, :256]
     db_rows = dot(wide_rows, onehot((256, 128), lambda a, b: b % 64 == 32 + a // 8), precision=highest)
     dfeat = ((da + da_recv[...] + db_rows) * mask).astype(bf16)
-    grads = dot(normed16, dfeat, ((0,), (0,)))
+    twice = dot(normed16, onehot((64, 128), lambda a, b: b % 64 == a).astype(bf16)).astype(bf16)
+    grads = dot(dfeat, twice, ((0,), (0,)))
     low = lax.broadcasted_iota(jnp.int32, (32, 128), 1) < 64
     small[0:32] = jnp.where(low, grads[0:32], grads[32:64]).astype(bf16)
     small[32:48] = jnp.broadcast_to(bias, (16, 128)).astype(bf16)
@@ -260,14 +270,16 @@
     def small_copy(dst, src):
         return pltpu.make_async_remote_copy(
             src_ref=small, dst_ref=small_recv.at[src], send_sem=wsend.at[dst], recv_sem=wrecv.at[src],
-            device_id=place(dst), device_id_type=MESH)
-
-    def send_small(k, carry):
-        small_copy(lax.rem(me + k, n), me).start()
-        return carry
-
-    lax.fori_loop(1, n, send_small, 0)
-    small_recv[me] = small[...]
+            device_id=place(layer * near + dst), device_id_type=MESH)
+
+    def plane_copy(dst, src):
+        return pltpu.make_async_remote_copy(
+            src_ref=plane, dst_ref=plane_recv.at[src], send_sem=vsend.at[dst], recv_sem=vrecv.at[src],
+            device_id=place(dst * near + spot), device_id_type=MESH)
+
+    for k in range(1, near):
+        small_copy(lax.rem(spot + k, near), spot).start()
+    small_recv[spot] = small[...]
 
     def wait_weight(k, carry):
         weight_copy(0, lax.rem(me + k, n)).wait_recv()
@@ -288,24 +300,32 @@
 
     lax.fori_loop(1, n, send_gather, 0)
 
-    dnormed = dot(dfeat, wab[...], ((1,), (1,)))
+    for k in range(1, near):
+        small_copy(0, lax.rem(spot + k, near)).wait_recv()
+    near_sum = small_recv[0].astype(f32)
+    for k in range(1, near):
+        near_sum = near_sum + small_recv[k].astype(f32)
+    plane[...] = near_sum.astype(bf16)
+    for k in range(1, far):
+        plane_copy(lax.rem(layer + k, far), layer).start()
+    plane_recv[layer] = plane[...]
+
+    dnormed = dot(dfeat, wab_t)
     rows_out[...] = inv_std * (
         dnormed - jnp.mean(dnormed, axis=-1, keepdims=True)
         - normed * jnp.mean(dnormed * normed, axis=-1, keepdims=True))
     for s in range(8):
         align[s] = rows_out[pl.ds(s, 16, stride=8), :]
 
-    def wait_small(k, carry):
-        small_copy(0, lax.rem(me + k, n)).wait_recv()
-        return carry
-
-    lax.fori_loop(1, n, wait_small, 0)
+    for k in range(1, far):
+        plane_copy(0, lax.rem(layer + k, far)).wait_recv()
     inv = 1.0 / (16 * nres)
-    sums = lax.fori_loop(1, n, lambda k, t: t + small_recv[k].astype(f32), small_recv[0].astype(f32)) * inv
-    wa_out[0:32] = sums[0:32, 0:32]
-    wa_out[32:64] = sums[0:32, 64:96]
-    wb_out[0:32] = sums[0:32, 32:64]
-    wb_out[32:64] = sums[0:32, 96:128]
+    sums = plane_recv[0].astype(f32)
+    for k in range(1, far):
+        sums = sums + plane_recv[k].astype(f32)
+    sums = sums * inv
+    wa_out[...] = sums[0:32, 0:64]
+    wb_out[...] = sums[0:32, 64:128]
     bias_out[...] = sums[32:33]
 
     def wait_gather(k, carry):
@@ -319,11 +339,15 @@
     def drain(k, carry):
         dst = lax.rem(me + k, n)
         weight_copy(dst, me).wait_send()
-        small_copy(dst, me).wait_send()
         gather_copy(dst, me).wait_send()
         return carry
 
     lax.fori_loop(1, n, drain, 0)
+
+    for k in range(1, near):
+        small_copy(lax.rem(spot + k, near), spot).wait_send()
+    for k in range(1, far):
+        plane_copy(lax.rem(layer + k, far), layer).wait_send()
 
     def drain_near(k, carry):
         @pl.when((k != 0) | (home != u))
@@ -337,6 +361,16 @@
         return carry
 
     lax.fori_loop(0, nres, drain_near, 0)
+
+
+def hand_over(*refs):
+    sems = refs[-1]
+    half = (len(refs) - 1) // 2
+    copies = [pltpu.make_async_copy(refs[k], refs[half + k], sems.at[k]) for k in range(half)]
+    for copy in copies:
+        copy.start()
+    for copy in copies:
+        copy.wait()
 
 
 def fused(
@@ -352,24 +386,28 @@
 ):
     bf16, f32 = jnp.bfloat16, jnp.float32
     n = nres * nsub
-    zeros = jnp.zeros((64, 64), bf16)
-    wab = jnp.concatenate([first_factor_matrix, second_factor_matrix, zeros], axis=1)
+    hbm = pl.BlockSpec(memory_space=pltpu.HBM)
     vmem = pl.BlockSpec(memory_space=pltpu.VMEM)
     dma = pltpu.SemaphoreType.DMA
+    shapes = (
+        jax.ShapeDtypeStruct((16, 128, 128), bf16),
+        jax.ShapeDtypeStruct((8, 16, 64), f32),
+        jax.ShapeDtypeStruct((32, 64), f32),
+        jax.ShapeDtypeStruct((32, 64), f32),
+        jax.ShapeDtypeStruct((1024, 128), f32),
+        jax.ShapeDtypeStruct((1, 128), f32),
+    )
+    operands = (
+        sequence_embedding, sequence_present_flags, position_couple_flags,
+        first_factor_matrix.T, second_factor_matrix.T,
+        final_linear_matrix, final_offset_vector.reshape(1, 128), couple_change_cotangent,
+    )
     outs = pl.pallas_call(
         functools.partial(kernel, nres, nsub),
-        out_shape=(
-            jax.ShapeDtypeStruct((16, 128, 128), bf16),
-            jax.ShapeDtypeStruct((8, 16, 64), f32),
-            jax.ShapeDtypeStruct((64, 32), f32),
-            jax.ShapeDtypeStruct((64, 32), f32),
-            jax.ShapeDtypeStruct((1024, 128), f32),
-            jax.ShapeDtypeStruct((1, 128), f32),
-        ),
-        in_specs=[vmem] * 6 + [pl.BlockSpec(memory_space=pl.ANY)],
+        out_shape=shapes,
+        in_specs=[hbm] * 8,
         out_specs=(vmem,) * 6,
-        scratch_shapes=[
-            pltpu.VMEM((16, 128, 128), f32),
+        scratch_shapes=[pltpu.VMEM(a.shape, a.dtype) for a in operands] + [
             pltpu.VMEM((128, 128), bf16),
             pltpu.VMEM((128, 128), bf16),
             pltpu.VMEM((16, 384), bf16),
@@ -379,7 +417,6 @@
             pltpu.VMEM((2, 256, 2048), bf16),
             pltpu.VMEM((128, 2048), bf16),
             pltpu.VMEM((2, 128, 4096), bf16),
-            pltpu.VMEM((8, 128), f32),
             pltpu.VMEM((nres, 16, 256), bf16),
             pltpu.VMEM((nres, 16, 256), bf16),
             pltpu.VMEM((n, 32, 128), bf16),
@@ -388,24 +425,32 @@
             pltpu.VMEM((128, 128), f32),
             pltpu.VMEM((128, 128), f32),
             pltpu.VMEM((48, 128), bf16),
-            pltpu.VMEM((n, 48, 128), bf16),
+            pltpu.VMEM((8, 48, 128), bf16),
+            pltpu.VMEM((48, 128), bf16),
+            pltpu.VMEM((n // 8, 48, 128), bf16),
             pltpu.VMEM((128, 64), f32),
-            dma,
+            dma((8,)),
             dma((nres,)), dma((nres,)),
             dma((nres,)), dma((nres,)),
             dma((n,)), dma((n,)),
             dma((n,)), dma((n,)),
-            dma((n,)), dma((n,)),
+            dma((8,)), dma((8,)),
             dma((2,)), dma((2,)),
+            dma((n // 8,)), dma((n // 8,)),
         ],
         compiler_params=pltpu.CompilerParams(
-            collective_id=0, has_side_effects=True, vmem_limit_bytes=48 * 1024 * 1024
+            collective_id=0, has_side_effects=True, vmem_limit_bytes=40 * 1024 * 1024
         ),
-    )(
-        sequence_embedding, sequence_present_flags, position_couple_flags, wab,
-        final_linear_matrix, final_offset_vector.reshape(1, 128), couple_change_cotangent,
-    )
-    return (*outs[:5], outs[5].reshape(128))
+    )(*operands)
+    outs = pl.pallas_call(
+        hand_over,
+        out_shape=shapes,
+        in_specs=[vmem] * 6,
+        out_specs=(hbm,) * 6,
+        scratch_shapes=[dma((6,))],
+        compiler_params=pltpu.CompilerParams(vmem_limit_bytes=32 * 1024 * 1024),
+    )(*outs)
+    return (outs[0], outs[1], outs[2].T, outs[3].T, outs[4], outs[5].reshape(128))
 
 
 def body(

time: 52.6 us -> 47.7 us (0.907)
  Pallas kernels: 43.7 us -> 40.9 us
  local copies, waits for them, and re-layouts: 7.85 us -> 5.69 us
    pallas_call x1 -> x2, Pallas kernels: 43.7 us -> 40.9 us  [the longest x1 39.9 us: fused(): pl.pallas_call(functools.partial(kernel, nres, nsub), out_shape=shapes, i...]
    unnamed x22 -> x16, local copies, waits for them, and re-layouts: 7.77 us -> 5.69 us
where the time goes in v2:
time: 47.7 us; the launch traced here: 47.3 us
  Pallas kernels  40.9 us (86%)
  local copies, waits for them, and re-layouts  5.69 us (12%)
  between operations  0.67 us (1%)
    pallas_call x1, Pallas kernels, fused(): pl.pallas_call(functools.partial(kernel, nres, nsub), out_shape=shapes, i...  39.9 us
    unnamed x16, local copies, waits for them, and re-layouts  5.69 us
    pallas_call x1, Pallas kernels, fused(): pl.pallas_call(hand_over, out_shape=shapes, in_specs=[vmem] * 6, out_spec...  1.06 us

profile of v2, /device:TPU:0, one launch (start us, length us, event | category | flops | bytes accessed | tf_op | source)
XLA Modules:
  0.0 47.3 jit_solution(5964833459811959647)
XLA Ops:
  0.6 0.0 copy-start.6
  0.6 0.0 copy-start.7
  0.7 0.7 %copy-done.6 = s32[8,16]{1,0:T(8,128)S(1)} copy-done((s32[8,16]{1,0:T(8,128)S(1)}, s32[8,16]{1,0:T(8,128)}, u32[]{:S(2)}) %copy-start.6) | copy-done | bytes 536
  1.3 0.0 copy-done.7
  1.3 0.0 copy-start
  1.3 1.2 %copy-done = f32[16,128,128]{2,1,0:T(8,128)S(1)} copy-done((f32[16,128,128]{2,1,0:T(8,128)S(1)}, f32[16,128,128]{2,1,0:T(8,128)}, u32[]{:S(2)}) %copy-start) | copy-done | bytes 1048600
  2.6 0.0 copy-start.1
  2.6 0.9 %copy-done.1 = bf16[1024,128]{1,0:T(8,128)(2,1)S(1)} copy-done((bf16[1024,128]{1,0:T(8,128)(2,1)S(1)}, bf16[1024,128]{1,0:T(8,128)(2,1)}, u32[]{:S(2)}) %copy-start.1) | copy-done | bytes 262168
  3.5 0.0 copy-start.2
  3.5 0.8 %copy-done.2 = bf16[8,16,64]{2,1,0:T(8,128)(2,1)S(1)} copy-done((bf16[8,16,64]{2,1,0:T(8,128)(2,1)S(1)}, bf16[8,16,64]{2,1,0:T(8,128)(2,1)}, u32[]{:S(2)}) %copy-start.2) | copy-done | bytes 16408
  4.3 0.0 copy-start.3
  4.3 0.7 %copy-done.3 = s32[16,128]{1,0:T(8,128)S(1)} copy-done((s32[16,128]{1,0:T(8,128)S(1)}, s32[16,128]{1,0:T(8,128)}, u32[]{:S(2)}) %copy-start.3) | copy-done | bytes 8216
  5.0 0.0 copy-start.4
  5.0 0.7 %copy-done.4 = bf16[64,32]{0,1:T(8,128)(2,1)S(1)} copy-done((bf16[64,32]{0,1:T(8,128)(2,1)S(1)}, bf16[64,32]{0,1:T(8,128)(2,1)}, u32[]{:S(2)}) %copy-start.4) | copy-done | bytes 4120
  5.7 0.0 copy-start.5
  5.7 0.7 %copy-done.5 = bf16[64,32]{0,1:T(8,128)(2,1)S(1)} copy-done((bf16[64,32]{0,1:T(8,128)(2,1)S(1)}, bf16[64,32]{0,1:T(8,128)(2,1)}, u32[]{:S(2)}) %copy-start.5) | copy-done | bytes 4120
  6.4 39.9 %shard_map.127 = (bf16[16,128,128]{2,1,0:T(8,128)(2,1)S(1)}, f32[8,16,64]{2,1,0:T(8,128)S(1)}, f32[32,64]{1,0:T(8,128)S(1)}, f32[32,64]{1,0:T(8,128)S(1)}, f32[1...) custom-call(bf16[8,16,64]{2,1,0:T(8,128)(2,1)S(1)} %copy-done.2, s32[8,16]{1,0:T(8,128)S(1)} %copy-done.6, ...), custom_call_target="tpu_custom_call" | custom-call | tf_op jit(solution)/shard_map/pallas_call | solution.py:405
  46.2 1.1 %shard_map.128 = (bf16[16,128,128]{2,1,0:T(8,128)(2,1)}, f32[8,16,64]{2,1,0:T(8,128)}, f32[32,64]{1,0:T(8,128)}, f32[32,64]{1,0:T(8,128)}, f32[1024,128]{1,0:T(8,128)}, /*index=5*/f32[1,128]{1,0:T(1,128)}) custom-call(bf16[16,128,128]{2,1,0:T(8,128)(2,1)S(1)} %get-tuple-element.18.refs_0_, f32[8,16,64]{2,1,0:T(8,128)S(1)} %get-tuple-element.19.refs_1_, ...), custom_call_target="tpu_custom_call" | custom-call | tf_op jit(solution)/shard_map/pallas_call | solution.py:445
Async XLA Ops:
  0.6 0.7 %copy-start.6 = (s32[8,16]{1,0:T(8,128)S(1)}, s32[8,16]{1,0:T(8,128)}, u32[]{:S(2)}) copy-start(s32[8,16]{1,0:T(8,128)} %flags_hbm.1) | copy-start | bytes 1540
  0.6 0.7 %copy-start.7 = (f32[128]{0:T(128)S(1)}, f32[128]{0:T(128)}, u32[]{:S(2)}) copy-start(f32[128]{0:T(128)} %param.14) | copy-start | bytes 1540
  1.3 1.2 %copy-start = (f32[16,128,128]{2,1,0:T(8,128)S(1)}, f32[16,128,128]{2,1,0:T(8,128)}, u32[]{:S(2)}) copy-start(f32[16,128,128]{2,1,0:T(8,128)} %cot_hbm.1) | copy-start | bytes 3145732
  2.6 0.9 %copy-start.1 = (bf16[1024,128]{1,0:T(8,128)(2,1)S(1)}, bf16[1024,128]{1,0:T(8,128)(2,1)}, u32[]{:S(2)}) copy-start(bf16[1024,128]{1,0:T(8,128)(2,1)} %lin_hbm.1) | copy-start | bytes 786436
  3.5 0.8 %copy-start.2 = (bf16[8,16,64]{2,1,0:T(8,128)(2,1)S(1)}, bf16[8,16,64]{2,1,0:T(8,128)(2,1)}, u32[]{:S(2)}) copy-start(bf16[8,16,64]{2,1,0:T(8,128)(2,1)} %emb_hbm.1) | copy-start | bytes 49156
  4.3 0.7 %copy-start.3 = (s32[16,128]{1,0:T(8,128)S(1)}, s32[16,128]{1,0:T(8,128)}, u32[]{:S(2)}) copy-start(s32[16,128]{1,0:T(8,128)} %pflags_hbm.1) | copy-start | bytes 24580
  5.0 0.7 %copy-start.4 = (bf16[64,32]{0,1:T(8,128)(2,1)S(1)}, bf16[64,32]{0,1:T(8,128)(2,1)}, u32[]{:S(2)}) copy-start(bf16[64,32]{0,1:T(8,128)(2,1)} %param.11) | copy-start | bytes 12292
  5.7 0.7 %copy-start.5 = (bf16[64,32]{0,1:T(8,128)(2,1)S(1)}, bf16[64,32]{0,1:T(8,128)(2,1)}, u32[]{:S(2)}) copy-start(bf16[64,32]{0,1:T(8,128)(2,1)} %param.12) | copy-start | bytes 12292

commit v3 on v2

--- a/solution.py
+++ b/solution.py
@@ -24,10 +24,11 @@
 def kernel(
     nres, nsub,
     emb_hbm, flags_hbm, pflags_hbm, wa_hbm, wb_hbm, lin_hbm, offset_hbm, cot_hbm,
-    pair, align, wa_out, wb_out, lin_out, bias_out,
-    emb, flags, pflags, wa_t, wb_t, lin, offset, cot, feat, other, blk, bmat, wm, lin32, tmat, gmat, dmat, dstage, drecv,
-    ostage, orecv, ogather, da_send, da_recv, small, small_recv, plane, plane_recv, rows_out,
-    in_sem, bsend, brecv, dsend, drecv_sem, osend, orecv_sem, gsend, grecv, wsend, wrecv, psend, precv, vsend, vrecv,
+    pair_hbm, align_hbm, wa_hbm_out, wb_hbm_out, lin_hbm_out, bias_hbm_out,
+    emb, flags, pflags, wa_t, wb_t, lin, offset, cot,
+    pair, align, wa_out, wb_out, lin_out, bias_out, feat, other, blk, bmat, wm, lin32, tmat, gmat, dmat, dstage, drecv,
+    ostage, orecv, ogather, fstage, frecv, owned, da_send, da_recv, small, small_recv, plane, plane_recv, rows_out,
+    in_sem, out_sem, bsend, brecv, dsend, drecv_sem, osend, orecv_sem, gsend, grecv, wsend, wrecv, psend, precv, vsend, vrecv, fsend, frecv_sem, hsend, hrecv,
 ):
     bf16, f32 = jnp.bfloat16, jnp.float32
     n = nres * nsub
@@ -43,6 +44,12 @@
         for k, (a, b) in enumerate([
             (emb_hbm, emb), (flags_hbm, flags), (wa_hbm, wa_t), (wb_hbm, wb_t),
             (lin_hbm, lin), (pflags_hbm, pflags), (offset_hbm, offset), (cot_hbm, cot)])
+    ]
+    outs = [
+        pltpu.make_async_copy(a, b, out_sem.at[k])
+        for k, (a, b) in enumerate([
+            (pair, pair_hbm), (align, align_hbm), (wa_out, wa_hbm_out),
+            (wb_out, wb_hbm_out), (lin_out, lin_hbm_out), (bias_out, bias_hbm_out)])
     ]
     for copy in ins:
         copy.start()
@@ -213,19 +220,34 @@
         lanes = slice(q * 512, (q + 1) * 512)
         part = dot(at_mine, dmat[u, :, lanes]) + dot(at_other, dmat[1 - u, :, lanes])
         for k in range(4):
-            ostage[q * 4 + k] = part[:, k * 128:(k + 1) * 128].astype(bf16)
-
-    def weight_copy(dst, src):
+            d = q * 4 + k
+            rows = slice(d // near * 32, d // near * 32 + 32)
+            ostage[d % near, rows, :] = part[:, k * 128:(k + 1) * 128].astype(bf16)
+
+    def near_copy(dst, src):
         return pltpu.make_async_remote_copy(
             src_ref=ostage.at[dst], dst_ref=orecv.at[src], send_sem=osend.at[dst], recv_sem=orecv_sem.at[src],
-            device_id=place(dst), device_id_type=MESH)
-
-    def send_weight(k, carry):
-        weight_copy(lax.rem(me + k, n), me).start()
-        return carry
-
-    lax.fori_loop(1, n, send_weight, 0)
-    orecv[me] = ostage[me]
+            device_id=place(layer * near + dst), device_id_type=MESH)
+
+    def far_copy(dst, src):
+        return pltpu.make_async_remote_copy(
+            src_ref=fstage.at[dst], dst_ref=frecv.at[src], send_sem=fsend.at[dst], recv_sem=frecv_sem.at[src],
+            device_id=place(dst * near + spot), device_id_type=MESH)
+
+    def far_gather(dst, src):
+        rows = pl.ds(pl.multiple_of(src * 32, 32), 32)
+        return pltpu.make_async_remote_copy(
+            src_ref=owned, dst_ref=ogather.at[spot, rows, :], send_sem=hsend.at[dst], recv_sem=hrecv.at[src],
+            device_id=place(dst * near + spot), device_id_type=MESH)
+
+    def near_gather(dst, src):
+        return pltpu.make_async_remote_copy(
+            src_ref=ogather.at[spot], dst_ref=ogather.at[src], send_sem=gsend.at[dst], recv_sem=grecv.at[src],
+            device_id=place(layer * near + dst), device_id_type=MESH)
+
+    for k in range(1, near):
+        near_copy(lax.rem(spot + k, near), spot).start()
+    orecv[spot] = ostage[spot]
 
     da_send[...] = dot(dmat[1 - u], wm[...], ((1,), (1,)))
 
@@ -243,6 +265,18 @@
         for k in range(2):
             i = p * 2 + k
             pair[i] = ((z[:, k * 128:(k + 1) * 128] + offset[...]) * scale[:, i:i + 1]).astype(bf16)
+
+    outs[0].start()
+    for k in range(1, near):
+        near_copy(0, lax.rem(spot + k, near)).wait_recv()
+    near_total = orecv[0].astype(f32)
+    for k in range(1, near):
+        near_total = near_total + orecv[k].astype(f32)
+    for k in range(far):
+        fstage[k] = near_total[k * 32:(k + 1) * 32].astype(bf16)
+    for k in range(1, far):
+        far_copy(lax.rem(layer + k, far), layer).start()
+    frecv[layer] = fstage[layer]
 
     da_copy().wait()
 
@@ -281,24 +315,15 @@
         small_copy(lax.rem(spot + k, near), spot).start()
     small_recv[spot] = small[...]
 
-    def wait_weight(k, carry):
-        weight_copy(0, lax.rem(me + k, n)).wait_recv()
-        return carry
-
-    lax.fori_loop(1, n, wait_weight, 0)
-    owned = lax.fori_loop(1, n, lambda k, t: t + orecv[k].astype(f32), orecv[0].astype(f32))
-    ogather[me] = owned.astype(bf16)
-
-    def gather_copy(dst, src):
-        return pltpu.make_async_remote_copy(
-            src_ref=ogather.at[me], dst_ref=ogather.at[src], send_sem=gsend.at[dst], recv_sem=grecv.at[src],
-            device_id=place(dst), device_id_type=MESH)
-
-    def send_gather(k, carry):
-        gather_copy(lax.rem(me + k, n), me).start()
-        return carry
-
-    lax.fori_loop(1, n, send_gather, 0)
+    for k in range(1, far):
+        far_copy(0, lax.rem(layer + k, far)).wait_recv()
+    far_total = frecv[0].astype(f32)
+    for k in range(1, far):
+        far_total = far_total + frecv[k].astype(f32)
+    owned[...] = far_total.astype(bf16)
+    for k in range(1, far):
+        far_gather(lax.rem(layer + k, far), layer).start()
+    ogather[spot, pl.ds(pl.multiple_of(layer * 32, 32), 32), :] = far_total.astype(bf16)
 
     for k in range(1, near):
         small_copy(0, lax.rem(spot + k, near)).wait_recv()
@@ -309,6 +334,11 @@
     for k in range(1, far):
         plane_copy(lax.rem(layer + k, far), layer).start()
     plane_recv[layer] = plane[...]
+
+    for k in range(1, far):
+        far_gather(0, lax.rem(layer + k, far)).wait_recv()
+    for k in range(1, near):
+        near_gather(lax.rem(spot + k, near), spot).start()
 
     dnormed = dot(dfeat, wab_t)
     rows_out[...] = inv_std * (
@@ -317,6 +347,7 @@
     for s in range(8):
         align[s] = rows_out[pl.ds(s, 16, stride=8), :]
 
+    outs[1].start()
     for k in range(1, far):
         plane_copy(0, lax.rem(layer + k, far)).wait_recv()
     inv = 1.0 / (16 * nres)
@@ -327,27 +358,23 @@
     wa_out[...] = sums[0:32, 0:64]
     wb_out[...] = sums[0:32, 64:128]
     bias_out[...] = sums[32:33]
-
-    def wait_gather(k, carry):
-        gather_copy(0, lax.rem(me + k, n)).wait_recv()
-        return carry
-
-    lax.fori_loop(1, n, wait_gather, 0)
+    for copy in (outs[2], outs[3], outs[5]):
+        copy.start()
+
+    for k in range(1, near):
+        near_gather(0, lax.rem(spot + k, near)).wait_recv()
     for d in range(32):
-        lin_out[pl.ds(d, 32, stride=32), :] = ogather[d].astype(f32) * inv
-
-    def drain(k, carry):
-        dst = lax.rem(me + k, n)
-        weight_copy(dst, me).wait_send()
-        gather_copy(dst, me).wait_send()
-        return carry
-
-    lax.fori_loop(1, n, drain, 0)
+        lin_out[pl.ds(d, 32, stride=32), :] = ogather[d % near, d // near * 32:d // near * 32 + 32, :].astype(f32) * inv
+    outs[4].start()
 
     for k in range(1, near):
         small_copy(lax.rem(spot + k, near), spot).wait_send()
+        near_copy(lax.rem(spot + k, near), spot).wait_send()
+        near_gather(lax.rem(spot + k, near), spot).wait_send()
     for k in range(1, far):
         plane_copy(lax.rem(layer + k, far), layer).wait_send()
+        far_copy(lax.rem(layer + k, far), layer).wait_send()
+        far_gather(lax.rem(layer + k, far), layer).wait_send()
 
     def drain_near(k, carry):
         @pl.when((k != 0) | (home != u))
@@ -361,15 +388,22 @@
         return carry
 
     lax.fori_loop(0, nres, drain_near, 0)
+    for copy in outs:
+        copy.wait()
 
 
 def hand_over(*refs):
-    sems = refs[-1]
-    half = (len(refs) - 1) // 2
-    copies = [pltpu.make_async_copy(refs[k], refs[half + k], sems.at[k]) for k in range(half)]
-    for copy in copies:
+    count = (len(refs) - 2) // 3
+    take, give = refs[-2], refs[-1]
+    held = refs[2 * count:3 * count]
+    first = [pltpu.make_async_copy(refs[k], held[k], take.at[k]) for k in range(count)]
+    second = [pltpu.make_async_copy(held[k], refs[count + k], give.at[k]) for k in range(count)]
+    for copy in first:
         copy.start()
-    for copy in copies:
+    for k in range(count):
+        first[k].wait()
+        second[k].start()
+    for copy in second:
         copy.wait()
 
 
@@ -386,8 +420,7 @@
 ):
     bf16, f32 = jnp.bfloat16, jnp.float32
     n = nres * nsub
-    hbm = pl.BlockSpec(memory_space=pltpu.HBM)
-    vmem = pl.BlockSpec(memory_space=pltpu.VMEM)
+    anywhere = pl.BlockSpec(memory_space=pl.ANY)
     dma = pltpu.SemaphoreType.DMA
     shapes = (
         jax.ShapeDtypeStruct((16, 128, 128), bf16),
@@ -405,9 +438,9 @@
     outs = pl.pallas_call(
         functools.partial(kernel, nres, nsub),
         out_shape=shapes,
-        in_specs=[hbm] * 8,
-        out_specs=(vmem,) * 6,
-        scratch_shapes=[pltpu.VMEM(a.shape, a.dtype) for a in operands] + [
+        in_specs=[anywhere] * 8,
+        out_specs=(anywhere,) * 6,
+        scratch_shapes=[pltpu.VMEM(a.shape, a.dtype) for a in operands + shapes] + [
             pltpu.VMEM((128, 128), bf16),
             pltpu.VMEM((128, 128), bf16),
             pltpu.VMEM((16, 384), bf16),
@@ -419,9 +452,12 @@
             pltpu.VMEM((2, 128, 4096), bf16),
             pltpu.VMEM((nres, 16, 256), bf16),
             pltpu.VMEM((nres, 16, 256), bf16),
-            pltpu.VMEM((n, 32, 128), bf16),
-            pltpu.VMEM((n, 32, 128), bf16),
-            pltpu.VMEM((n, 32, 128), bf16),
+            pltpu.VMEM((8, n * 4, 128), bf16),
+            pltpu.VMEM((8, n * 4, 128), bf16),
+            pltpu.VMEM((8, n * 4, 128), bf16),
+            pltpu.VMEM((n // 8, 32, 128), bf16),
+            pltpu.VMEM((n // 8, 32, 128), bf16),
+            pltpu.VMEM((32, 128), bf16),
             pltpu.VMEM((128, 128), f32),
             pltpu.VMEM((128, 128), f32),
             pltpu.VMEM((48, 128), bf16),
@@ -429,26 +465,28 @@
             pltpu.VMEM((48, 128), bf16),
             pltpu.VMEM((n // 8, 48, 128), bf16),
             pltpu.VMEM((128, 64), f32),
-            dma((8,)),
+            dma((8,)), dma((6,)),
             dma((nres,)), dma((nres,)),
             dma((nres,)), dma((nres,)),
-            dma((n,)), dma((n,)),
-            dma((n,)), dma((n,)),
+            dma((8,)), dma((8,)),
+            dma((8,)), dma((8,)),
             dma((8,)), dma((8,)),
             dma((2,)), dma((2,)),
             dma((n // 8,)), dma((n // 8,)),
+            dma((n // 8,)), dma((n // 8,)),
+            dma((n // 8,)), dma((n // 8,)),
         ],
         compiler_params=pltpu.CompilerParams(
-            collective_id=0, has_side_effects=True, vmem_limit_bytes=40 * 1024 * 1024
+            collective_id=0, has_side_effects=True, vmem_limit_bytes=60 * 1024 * 1024
         ),
     )(*operands)
     outs = pl.pallas_call(
         hand_over,
         out_shape=shapes,
-        in_specs=[vmem] * 6,
-        out_specs=(hbm,) * 6,
-        scratch_shapes=[dma((6,))],
-        compiler_params=pltpu.CompilerParams(vmem_limit_bytes=32 * 1024 * 1024),
+        in_specs=[anywhere] * 6,
+        out_specs=(anywhere,) * 6,
+        scratch_shapes=[pltpu.VMEM(a.shape, a.dtype) for a in shapes] + [dma((6,)), dma((6,))],
+        compiler_params=pltpu.CompilerParams(vmem_limit_bytes=60 * 1024 * 1024),
     )(*outs)
     return (outs[0], outs[1], outs[2].T, outs[3].T, outs[4], outs[5].reshape(128))
 

time: 47.7 us -> 38 us (0.80)
  local copies, waits for them, and re-layouts: 5.69 us -> 0 us
  Pallas kernels: 40.9 us -> 37.2 us
    unnamed x16 -> x0, local copies, waits for them, and re-layouts: 5.69 us -> none
    pallas_call x1, Pallas kernels: 39.9 us -> 35.1 us  [fused(): pl.pallas_call(functools.partial(kernel, nres, nsub), out_shape=shapes, i...]
    pallas_call x1, Pallas kernels: 1.06 us -> 2.15 us  [fused(): pl.pallas_call(hand_over, out_shape=shapes, in_specs=[anywhere] * 6, out_...]
where the time goes in v3:
time: 38 us; the launch traced here: 37.9 us
  Pallas kernels  37.2 us (98%)
  between operations  0.64 us (2%)
    pallas_call x1, Pallas kernels, fused(): pl.pallas_call(functools.partial(kernel, nres, nsub), out_shape=shapes, i...  35.1 us
    pallas_call x1, Pallas kernels, fused(): pl.pallas_call(hand_over, out_shape=shapes, in_specs=[anywhere] * 6, out_...  2.15 us

profile of v3, /device:TPU:0, one launch (start us, length us, event | category | flops | bytes accessed | tf_op | source)
XLA Modules:
  0.0 37.9 jit_solution(3939452962495601176)
XLA Ops:
  0.6 35.1 %shard_map.127 = (bf16[16,128,128]{2,1,0:T(8,128)(2,1)}, f32[8,16,64]{2,1,0:T(8,128)}, f32[32,64]{1,0:T(8,128)}, f32[32,64]{1,0:T(8,128)}, f32[1024,128]{1,0:T(8,128)}, /*index=5*/f32[1,128]{1,0:T(1,128)}) custom-call(bf16[8,16,64]{2,1,0:T(8,128)(2,1)} %emb_hbm.1, s32[8,16]{1,0:T(8,128)} %flags_hbm.1, s32[16,128]{1,0:T(8,128)} %pflags_hbm.1, ...), custom_call_target="tpu_custom_call" | custom-call | tf_op jit(solution)/shard_map/pallas_call | solution.py:438
  35.7 2.2 %shard_map.128 = (bf16[16,128,128]{2,1,0:T(8,128)(2,1)}, f32[8,16,64]{2,1,0:T(8,128)}, f32[32,64]{1,0:T(8,128)}, f32[32,64]{1,0:T(8,128)}, f32[1024,128]{1,0:T(8,128)}, /*index=5*/f32[1,128]{1,0:T(1,128)}) custom-call(bf16[16,128,128]{2,1,0:T(8,128)(2,1)} %get-tuple-element.18.refs_0_, f32[8,16,64]{2,1,0:T(8,128)} %get-tuple-element.19.refs_1_, ...), custom_call_target="tpu_custom_call" | custom-call | tf_op jit(solution)/shard_map/pallas_call | solution.py:483

commit v4 on v3

--- a/solution.py
+++ b/solution.py
@@ -96,17 +96,23 @@
 
     partner_copy().start()
 
+    core = lax.rem(r, 2)
+    chips = nres // 2
+    spot_in = lax.rem(r, nblk) // 2
+
     def block_copy(k):
-        q = lax.rem(r + k, nres)
-        return pltpu.make_async_remote_copy(
-            src_ref=blk, dst_ref=bmat.at[u, rows_here, :], send_sem=bsend.at[k], recv_sem=brecv.at[slot],
+        q = lax.rem(r // 2 + k, chips) * 2 + core
+        return pltpu.make_async_remote_copy(
+            src_ref=blk, dst_ref=bmat.at[u, spot_in, core], send_sem=bsend.at[k], recv_sem=brecv.at[slot // 2],
             device_id={"res": q, "sub": home}, device_id_type=MESH)
 
-    def send_block(k, carry):
+    def pass_copy(which):
+        return pltpu.make_async_remote_copy(
+            src_ref=bmat.at[:, :, core], dst_ref=bmat.at[:, :, which], send_sem=bsend.at[chips], recv_sem=brecv.at[chips],
+            device_id={"res": r // 2 * 2 + 1 - core, "sub": u}, device_id_type=MESH)
+
+    for k in range(1, chips):
         block_copy(k).start()
-        return carry
-
-    lax.fori_loop(1, nres, send_block, 0)
 
     @pl.when(home != u)
     def _():
@@ -114,7 +120,7 @@
 
     @pl.when(home == u)
     def _():
-        bmat[u, rows_here, :] = mine
+        bmat[u, spot_in, core] = mine
 
     ins[4].wait()
     lin32[...] = lin[...].astype(f32)
@@ -140,6 +146,16 @@
     mine_left = left_only(feat)
     mix(u, mine_left.astype(bf16))
     partner_copy().wait()
+    for k in range(chips):
+        copy = pltpu.make_async_remote_copy(
+            src_ref=blk, dst_ref=bmat.at[k // (nblk // 2), k % (nblk // 2), core], send_sem=bsend.at[0],
+            recv_sem=brecv.at[k], device_id={"res": r, "sub": 1 - u}, device_id_type=MESH)
+
+        @pl.when((slot // 2 != k) | (home != u))
+        def _():
+            copy.wait_recv()
+
+    pass_copy(core).start()
     other_left = left_only(other)
     mix(1 - u, other_left.astype(bf16))
 
@@ -148,26 +164,12 @@
     for copy in ins[5:]:
         copy.wait()
 
-    def wait_block(k, carry):
-        @pl.when(k != slot)
-        def _():
-            copy = pltpu.make_async_remote_copy(
-                src_ref=blk, dst_ref=bmat.at[k // nblk, pl.ds(pl.multiple_of(lax.rem(k, nblk) * 16, 16), 16), :],
-                send_sem=bsend.at[0], recv_sem=brecv.at[k], device_id={"res": r, "sub": 1 - u}, device_id_type=MESH)
-            copy.wait_recv()
-
-        @pl.when((k == slot) & (home != u))
-        def _():
-            copy = pltpu.make_async_remote_copy(
-                src_ref=blk, dst_ref=bmat.at[k // nblk, pl.ds(pl.multiple_of(lax.rem(k, nblk) * 16, 16), 16), :],
-                send_sem=bsend.at[0], recv_sem=brecv.at[k], device_id={"res": r, "sub": 1 - u}, device_id_type=MESH)
-            copy.wait_recv()
-
-        return carry
-
-    lax.fori_loop(0, nres, wait_block, 0)
-
-    count = dot(mask_rows[0], bmat[u, :, 256:384], ((1,), (1,))) + dot(mask_rows[1], bmat[1 - u, :, 256:384], ((1,), (1,)))
+    pass_copy(1 - core).wait_recv()
+
+    def cols(half):
+        return bmat[half].reshape(128, 384)
+
+    count = dot(mask_rows[0], cols(u)[:, 256:384], ((1,), (1,))) + dot(mask_rows[1], cols(1 - u)[:, 256:384], ((1,), (1,)))
     scale = (pflags[...].astype(f32) / jnp.maximum(count, 1.0)).T
     bias = jnp.zeros((1, 128), f32)
     for i in range(16):
@@ -203,7 +205,7 @@
 
     lax.fori_loop(0, nres, send_grad, 0)
 
-    bt = [bmat[half, :, 0:256].astype(f32).T.astype(bf16) for half in range(2)]
+    bt = [cols(half)[:, 0:256].astype(f32).T.astype(bf16) for half in range(2)]
 
     for p in range(8):
         g = gmat[:, p * 256:(p + 1) * 256]
@@ -249,7 +251,7 @@
         near_copy(lax.rem(spot + k, near), spot).start()
     orecv[spot] = ostage[spot]
 
-    da_send[...] = dot(dmat[1 - u], wm[...], ((1,), (1,)))
+    da_send[...] = dot(dmat[1 - u], wm[...], ((1,), (1,))).astype(bf16)
 
     def da_copy():
         return pltpu.make_async_remote_copy(
@@ -261,7 +263,7 @@
 
     for p in range(8):
         lanes = slice(p * 256, (p + 1) * 256)
-        z = dot(bmat[0, :, 0:256], tmat[0, :, lanes]) + dot(bmat[1, :, 0:256], tmat[1, :, lanes])
+        z = dot(cols(0)[:, 0:256], tmat[0, :, lanes]) + dot(cols(1)[:, 0:256], tmat[1, :, lanes])
         for k in range(2):
             i = p * 2 + k
             pair[i] = ((z[:, k * 128:(k + 1) * 128] + offset[...]) * scale[:, i:i + 1]).astype(bf16)
@@ -294,7 +296,7 @@
     highest = lax.Precision.HIGHEST
     wide_rows = dot(onehot((128, 16), lambda a, b: a // 8 == b), total, precision=highest) * keep[:, :256]
     db_rows = dot(wide_rows, onehot((256, 128), lambda a, b: b % 64 == 32 + a // 8), precision=highest)
-    dfeat = ((da + da_recv[...] + db_rows) * mask).astype(bf16)
+    dfeat = ((da + da_recv[...].astype(f32) + db_rows) * mask).astype(bf16)
     twice = dot(normed16, onehot((64, 128), lambda a, b: b % 64 == a).astype(bf16)).astype(bf16)
     grads = dot(dfeat, twice, ((0,), (0,)))
     low = lax.broadcasted_iota(jnp.int32, (32, 128), 1) < 64
@@ -377,10 +379,6 @@
         far_gather(lax.rem(layer + k, far), layer).wait_send()
 
     def drain_near(k, carry):
-        @pl.when((k != 0) | (home != u))
-        def _():
-            block_copy(k).wait_send()
-
         @pl.when(jnp.logical_not(is_self(k)))
         def _():
             grad_copy(r, k).wait_send()
@@ -388,6 +386,14 @@
         return carry
 
     lax.fori_loop(0, nres, drain_near, 0)
+    for k in range(1, chips):
+        block_copy(k).wait_send()
+
+    @pl.when(home != u)
+    def _():
+        block_copy(0).wait_send()
+
+    pass_copy(core).wait_send()
     for copy in outs:
         copy.wait()
 
@@ -444,7 +450,7 @@
             pltpu.VMEM((128, 128), bf16),
             pltpu.VMEM((128, 128), bf16),
             pltpu.VMEM((16, 384), bf16),
-            pltpu.VMEM((2, 128, 384), bf16),
+            pltpu.VMEM((2, nres // 4, 2, 16, 384), bf16),
             pltpu.VMEM((128, 4096), bf16),
             pltpu.VMEM((1024, 128), f32),
             pltpu.VMEM((2, 256, 2048), bf16),
@@ -458,8 +464,8 @@
             pltpu.VMEM((n // 8, 32, 128), bf16),
             pltpu.VMEM((n // 8, 32, 128), bf16),
             pltpu.VMEM((32, 128), bf16),
-            pltpu.VMEM((128, 128), f32),
-            pltpu.VMEM((128, 128), f32),
+            pltpu.VMEM((128, 128), bf16),
+            pltpu.VMEM((128, 128), bf16),
             pltpu.VMEM((48, 128), bf16),
             pltpu.VMEM((8, 48, 128), bf16),
             pltpu.VMEM((48, 128), bf16),

time: 38 us -> 37.5 us (0.987)
  Pallas kernels: 37.2 us -> 36.7 us
    pallas_call x1, Pallas kernels: 35.1 us -> 34.5 us  [fused(): pl.pallas_call(functools.partial(kernel, nres, nsub), out_shape=shapes, i...]
where the time goes in v4:
time: 37.5 us; the launch traced here: 37.3 us
  Pallas kernels  36.7 us (98%)
  between operations  0.64 us (2%)
    pallas_call x1, Pallas kernels, fused(): pl.pallas_call(functools.partial(kernel, nres, nsub), out_shape=shapes, i...  34.5 us
    pallas_call x1, Pallas kernels, fused(): pl.pallas_call(hand_over, out_shape=shapes, in_specs=[anywhere] * 6, out_...  2.15 us

profile of v4, /device:TPU:0, one launch (start us, length us, event | category | flops | bytes accessed | tf_op | source)
XLA Modules:
  0.0 37.3 jit_solution(13296121803191664514)
XLA Ops:
  0.6 34.5 %shard_map.127 = (bf16[16,128,128]{2,1,0:T(8,128)(2,1)}, f32[8,16,64]{2,1,0:T(8,128)}, f32[32,64]{1,0:T(8,128)}, f32[32,64]{1,0:T(8,128)}, f32[1024,128]{1,0:T(8,128)}, /*index=5*/f32[1,128]{1,0:T(1,128)}) custom-call(bf16[8,16,64]{2,1,0:T(8,128)(2,1)} %emb_hbm.1, s32[8,16]{1,0:T(8,128)} %flags_hbm.1, s32[16,128]{1,0:T(8,128)} %pflags_hbm.1, ...), custom_call_target="tpu_custom_call" | custom-call | tf_op jit(solution)/shard_map/pallas_call | solution.py:444
  35.1 2.2 %shard_map.128 = (bf16[16,128,128]{2,1,0:T(8,128)(2,1)}, f32[8,16,64]{2,1,0:T(8,128)}, f32[32,64]{1,0:T(8,128)}, f32[32,64]{1,0:T(8,128)}, f32[1024,128]{1,0:T(8,128)}, /*index=5*/f32[1,128]{1,0:T(1,128)}) custom-call(bf16[16,128,128]{2,1,0:T(8,128)(2,1)} %get-tuple-element.18.refs_0_, f32[8,16,64]{2,1,0:T(8,128)} %get-tuple-element.19.refs_1_, ...), custom_call_target="tpu_custom_call" | custom-call | tf_op jit(solution)/shard_map/pallas_call | solution.py:489
